TPU v7x, 128 devices: a whole 4x4x4 slice. The times are simulated.
128 devices in a mesh: expert: 32 (over z, y, x_hi), replica: 4 (over x_lo, core).
Axes of the slice: x: 4 (x_hi: 2, x_lo: 2; x = x_hi * 2 + x_lo), y: 4, z: 4, core: 2. Of those that a mesh axis runs over, the one named last changes fastest.
Arguments:
- tokens: bfloat16 [16384, 2048], P(('expert', 'replica')), may hold values from -6 to 6
- expert_ids: int32 [16384, 10], P(('expert', 'replica')), may hold values from 0 to 255, all different within a row; in each aligned block of 128 rows (0 to 127, 128 to 255, ...) at most 6 rows name the same one
- router_scores: float32 [16384, 10], P(('expert', 'replica')), may hold values from -8 to 320
- lane_list: int32 [256], replicated, may hold values from 0 to 7, as said below
- capacity: int32 [256], replicated, may hold values from 320 to 640, as said below
- train_gate: bfloat16 [256, 2048, 512], P('expert', 'replica'), may hold values from -0.125 to 0.125
- train_up: bfloat16 [256, 2048, 512], P('expert', 'replica'), may hold values from -0.125 to 0.125
- train_down: bfloat16 [256, 2048, 512], P('expert', 'replica'), may hold values from -0.25 to 0.25
Outputs:
- combined: bfloat16 [16384, 2048], P(('expert', 'replica'))
- rollout_gate: bfloat16 [256, 2048, 512], P(('expert', 'replica'))
- rollout_up: bfloat16 [256, 2048, 512], P(('expert', 'replica'))
- rollout_down: bfloat16 [256, 2048, 512], P(('expert', 'replica'))
Inputs may be any that keep to these rules, and one draw needn't show every extreme that they name: `expert_ids`: among the 128 tokens of one device no expert is named by more than 6 tokens, and some device names some expert exactly 6 times. `lane_list`: each run of 8 entries that starts at a multiple of 8 holds each of 0 to 7 once. Some expert has capacity exactly 640.
All inputs are finite; a program needn't handle non-finite values.
Results may differ from a plain program's by a relative error of at most 0.0058.
Values may be sent and summed in bfloat16 or wider, within the bound.
A program may use at most 128 MiB of HBM per device.

v0:
```python
import jax
import jax.numpy as jnp
from jax import lax
from jax.sharding import PartitionSpec as P


def local(tokens, expert_ids, router_scores, lane_list, capacity, train_gate, train_up, train_down):
    n_expert = lax.axis_size("expert")
    n_replica = lax.axis_size("replica")
    lane_count = train_gate.shape[0]
    per_device = lane_count // n_replica
    device_count = n_expert * n_replica
    expert_total = lane_count * n_expert
    tok_count = tokens.shape[0]
    top_count = expert_ids.shape[1]
    width = tokens.shape[1]
    slot_cap = max(2, tok_count * top_count // expert_total + 1)
    column = lax.axis_index("expert")
    own_lanes = lax.dynamic_slice_in_dim(lane_list, column * lane_count, lane_count)
    lane_range = jnp.arange(lane_count, dtype=jnp.int32)
    source_slot = jnp.sum(
        jnp.where(own_lanes[None, :] == lane_range[:, None], lane_range[None, :], 0), axis=1
    )
    ordered = tuple(
        (jnp.take(weight, source_slot, axis=0) for weight in (train_gate, train_up, train_down))
    )
    rollout = (
        lax.all_to_all(ordered[0], "replica", split_axis=0, concat_axis=1, tiled=True),
        lax.all_to_all(ordered[1], "replica", split_axis=0, concat_axis=1, tiled=True),
        lax.all_to_all(ordered[2], "replica", split_axis=0, concat_axis=1, tiled=True),
    )
    expert_range = jnp.arange(expert_total, dtype=jnp.int32)
    slot_of = expert_range // lane_count * lane_count + lane_list
    expert_hits = (expert_ids[:, :, None] == expert_range[None, None, :]).astype(jnp.int32)
    per_token = jnp.sum(expert_hits, axis=1)
    before = jnp.cumsum(per_token, axis=0) - per_token
    place_index = jnp.sum(expert_hits * before[:, None, :], axis=2)
    slot_ids = jnp.sum(expert_hits * slot_of[None, None, :], axis=2)
    counts = jnp.sum(per_token, axis=0)
    flat_index = (slot_ids * slot_cap + place_index).reshape(-1)
    token_index = jnp.broadcast_to(
        jnp.arange(tok_count, dtype=jnp.int32)[:, None], (tok_count, top_count)
    ).reshape(-1)
    row_source = jnp.zeros((expert_total * slot_cap,), jnp.int32).at[flat_index].set(token_index)
    filled = jnp.zeros((expert_total * slot_cap,), jnp.int32).at[flat_index].set(1)
    send_rows = jnp.where(
        filled[:, None] > 0, jnp.take(tokens, row_source, axis=0), jnp.zeros((), tokens.dtype)
    )
    send_counts = jnp.zeros((expert_total,), jnp.int32).at[slot_of].set(counts)
    joint_rows = send_rows.reshape(device_count, per_device, slot_cap, width)
    joint_counts = send_counts.reshape(device_count, per_device, 1)
    recv_rows, recv_counts = (
        lax.all_to_all(joint_rows, ("expert", "replica"), split_axis=0, concat_axis=2, tiled=True),
        lax.all_to_all(
            joint_counts, ("expert", "replica"), split_axis=0, concat_axis=2, tiled=True
        ),
    )
    recv_rows = recv_rows.reshape(per_device, device_count * slot_cap, width)
    recv_counts = recv_counts.reshape(per_device, device_count)
    device_index = column * n_replica + lax.axis_index("replica")
    own_slots = device_index * per_device + jnp.arange(per_device, dtype=jnp.int32)
    own_cap = jnp.sum(
        jnp.where(slot_of[None, :] == own_slots[:, None], capacity[None, :], 0), axis=1
    )
    earlier = jnp.cumsum(recv_counts, axis=1) - recv_counts
    position = jnp.arange(slot_cap, dtype=jnp.int32)
    arrival_rank = earlier[:, :, None] + position[None, None, :]
    kept_rows = (position[None, None, :] < recv_counts[:, :, None]) & (
        arrival_rank < own_cap[:, None, None]
    )
    kept_rows = kept_rows.reshape(per_device, device_count * slot_cap)
    gate_part = jnp.einsum(
        "scd,sdh->sch", recv_rows, rollout[0], preferred_element_type=jnp.float32
    )
    up_part = jnp.einsum("scd,sdh->sch", recv_rows, rollout[1], preferred_element_type=jnp.float32)
    hidden = (jax.nn.silu(gate_part) * up_part).astype(jnp.bfloat16)
    result = jnp.einsum("sch,sdh->scd", hidden, rollout[2], preferred_element_type=jnp.float32)
    result = jnp.where(kept_rows[..., None], result, 0.0).astype(jnp.bfloat16)
    joint_result = result.reshape(1, per_device, device_count * slot_cap, width)
    returned = lax.all_to_all(
        joint_result, ("expert", "replica"), split_axis=2, concat_axis=0, tiled=True
    )
    returned = returned.reshape(expert_total * slot_cap, width)
    picked = jnp.take(returned, flat_index, axis=0).reshape(tok_count, top_count, width)
    gates = jax.nn.softmax(router_scores, axis=-1)
    combined = jnp.sum(gates[:, :, None] * picked.astype(jnp.float32), axis=1).astype(jnp.bfloat16)
    return (combined, rollout[0], rollout[1], rollout[2])


def solution(mesh):
    placed = (
        P(("expert", "replica"), None),
        P(("expert", "replica"), None),
        P(("expert", "replica"), None),
        P(),
        P(),
        P("expert", "replica", None),
        P("expert", "replica", None),
        P("expert", "replica", None),
    )
    return jax.shard_map(
        local,
        mesh=mesh,
        in_specs=placed,
        out_specs=(
            P(("expert", "replica"), None),
            P(("expert", "replica"), None, None),
            P(("expert", "replica"), None, None),
            P(("expert", "replica"), None, None),
        ),
        check_vma=False,
    )
```

profile of v0, /device:TPU:1, one launch (start us, length us, event | category | flops | bytes accessed | tf_op | source)
XLA Modules:
  0.0 463.6 jit_solution(5660766478881993850)
XLA Ops:
  0.6 1.0 convert_reduce_fusion.1
  1.7 0.2 reduce_window_sum.22
  1.9 0.7 compare_select_fusion.4
  2.5 1.5 select_reduce_fusion.1
  4.0 1.4 scatter_custom_fusion
  5.4 0.8 reshape.174
  6.2 11.5 %all-to-all-start = ((s32[128,2,1]{1,2,0:T(1,128)}), s32[128,2,1]{1,2,0:T(1,128)S(1)}, u32[]{:S(2)}, u32[]{:S(2)}) async-start(s32[128,2,1]{1,2,0:T(1,128)} %bitcast), calls=%async_computation | async-start | bytes 131072 | tf_op jit(solution)/shard_map/all_to_all | solution.py:54
  17.7 0.8 dynamic_slice.3
  18.5 0.1 select_reduce_fusion.2
  18.6 5.0 %gather_fusion.2 = bf16[8,512,512]{2,1,0:T(8,128)(2,1)} fusion(bf16[8,512,512]{2,1,0:T(8,128)(2,1)} %param.15, s32[1024]{0:T(1024)S(1)} %pad_clamp_fusion.2), kind=kCustom, calls=%fused_computation.clone | custom fusion | bytes 8388640 | tf_op jit(solution)/shard_map/jit(_take)/gather | solution.py:25
  23.7 5.0 %gather_fusion.3 = bf16[8,512,512]{2,1,0:T(8,128)(2,1)} fusion(bf16[8,512,512]{2,1,0:T(8,128)(2,1)} %param.16, s32[1024]{0:T(1024)S(1)} %pad_clamp_fusion.2), kind=kCustom, calls=%fused_computation.1.clone | custom fusion | bytes 8388640 | tf_op jit(solution)/shard_map/jit(_take)/gather | solution.py:25
  28.7 5.0 %gather_fusion.4 = bf16[8,512,512]{2,1,0:T(8,128)(2,1)} fusion(bf16[8,512,512]{2,1,0:T(8,128)(2,1)} %param.17, s32[1024]{0:T(1024)S(1)} %pad_clamp_fusion.2), kind=kCustom, calls=%fused_computation.2.clone | custom fusion | bytes 8388640 | tf_op jit(solution)/shard_map/jit(_take)/gather | solution.py:25
  33.7 8.9 %broadcast_select_fusion.1 = (bf16[8,512,512]{2,1,0:T(8,128)(2,1)}, bf16[8,512,512]{2,1,0:T(8,128)(2,1)}, bf16[8,512,512]{2,1,0:T(8,128)(2,1)}) fusion(bf16[8,512,512]{2,1,0:T(8,128)(2,1)} %gather_fusion.3, pred[8]{0:T(512)(128)(4,1)S(1)} %compare_and_fusion.3, bf16[8,512,512]{2,1,0:T(8,128)(2,1)} %gather_fusion.4, bf16[8,512,512]{2,1,0:T(8,128)(2,1)} %gather_fusion.2), kind=kLoop, calls=%fused_computation.17 | loop fusion | flops 6291456 | bytes 25165832 | tf_op jit(solution)/shard_map/jit(_take)/select_n | solution.py:25
  42.6 54.2 %all_to_all.99 = bf16[8,512,512]{2,1,0:T(8,128)(2,1)} all-to-all(bf16[8,512,512]{2,1,0:T(8,128)(2,1)} %get-tuple-element.14), channel_id=1, replica_groups=mesh['expert'=32,'replica'=4] {'replica'}, dimensions={0} | all-to-all | bytes 8388608 | tf_op jit(solution)/shard_map/all_to_all | solution.py:28
  96.8 51.6 %all_to_all.100 = bf16[8,512,512]{2,1,0:T(8,128)(2,1)} all-to-all(bf16[8,512,512]{2,1,0:T(8,128)(2,1)S(1)} %copy-done.3), channel_id=1, replica_groups=mesh['expert'=32,'replica'=4] {'replica'}, dimensions={0} | all-to-all | bytes 8388608 | tf_op jit(solution)/shard_map/all_to_all | solution.py:29
  148.4 5.8 %all-to-all-start.4 = ((bf16[8,512,512]{2,1,0:T(8,128)(2,1)}), bf16[8,512,512]{2,1,0:T(8,128)(2,1)}, u32[]{:S(2)}, u32[]{:S(2)}) async-start(bf16[8,512,512]{2,1,0:T(8,128)(2,1)} %get-tuple-element.13), calls=%async_computation.4 | async-start | bytes 8388608 | tf_op jit(solution)/shard_map/all_to_all | solution.py:30
  154.4 0.1 add.111
  154.5 0.1 reshape.239
  154.7 5.2 %scatter_custom_fusion.2 = s32[1536]{0:T(1024)S(1)} fusion(s32[1280]{0:T(1024)S(1)} %fusion.12, s32[1280]{0:T(1024)S(1)} %reshape.239, s32[]{:T(128)} %constant.57.clone.1), kind=kCustom, calls=%fused_computation.42 | custom fusion | bytes 6148 | tf_op jit(solution)/shard_map/scatter | solution.py:44
  160.0 7.1 %gather_fusion = bf16[1536,2048]{1,0:T(8,128)(2,1)} fusion(bf16[128,2048]{1,0:T(8,128)(2,1)S(1)} %copy-done, s32[2048]{0:T(1024)S(1)} %pad_clamp_fusion.1), kind=kCustom, calls=%fused_computation.3 | custom fusion | bytes 12589056 | tf_op jit(solution)/shard_map/jit(_take)/gather | solution.py:47
  167.1 10.9 %gather.16 = bf16[128,2,6,2048]{3,2,1,0:T(8,128)(2,1)} reshape(bf16[1536,2048]{1,0:T(8,128)(2,1)} %gather_fusion) | data formatting | bytes 12582912 | tf_op jit(solution)/shard_map/jit(_take)/gather | solution.py:47
  178.0 0.2 broadcast_in_dim.124
  178.2 5.2 %scatter_custom_fusion.1 = s32[1536]{0:T(1024)S(1)} fusion(s32[1280]{0:T(1024)S(1)} %fusion.12, s32[1280]{0:T(1024)S(1)} %broadcast.131, s32[]{:T(128)} %constant.57.clone.1), kind=kCustom, calls=%fused_computation.45 | custom fusion | bytes 6148 | tf_op jit(solution)/shard_map/scatter | solution.py:45
  183.5 0.2 broadcast_in_dim.121
  183.7 4.8 %select_select_fusion = bf16[128,2,6,2048]{3,2,1,0:T(8,128)(2,1)S(1)} fusion(bf16[128,2,6,2048]{3,2,1,0:T(8,128)(2,1)} %gather.16, pred[128,2,6]{2,1,0:T(4,128)(4,1)S(1)} %broadcast_in_dim.124, pred[128,2,6]{2,1,0:T(4,128)(4,1)S(1)} %broadcast_in_dim.121), kind=kLoop, calls=%fused_computation.10 | loop fusion | flops 6291456 | bytes 12585984 | tf_op jit(solution)/shard_map/jit(_where)/select_n | solution.py:46
  188.5 15.2 %copy.46 = bf16[128,2,6,2048]{3,1,2,0:T(2,128)(2,1)} copy(bf16[128,2,6,2048]{3,2,1,0:T(8,128)(2,1)S(1)} %select_select_fusion) | data formatting | bytes 12582912 | tf_op jit(solution)/shard_map/jit(_where)/select_n | solution.py:46
  203.7 9.7 %all-to-all-start.1 = ((bf16[128,2,6,2048]{3,1,2,0:T(2,128)(2,1)}), bf16[128,2,6,2048]{3,1,2,0:T(2,128)(2,1)}, u32[]{:S(2)}, u32[]{:S(2)}) async-start(bf16[128,2,6,2048]{3,1,2,0:T(2,128)(2,1)} %copy.46), calls=%async_computation.1 | async-start | bytes 12582912 | tf_op jit(solution)/shard_map/all_to_all | solution.py:53
  213.4 0.1 lt.85
  213.5 0.2 fusion.17
  213.8 0.3 reduce_window_sum.23
  214.2 0.2 add.106
  214.5 0.2 lt.90
  214.7 4.6 %copy.47 = bf16[4,2,512,512]{3,2,0,1:T(8,128)(2,1)} copy(bf16[4,2,512,512]{3,2,1,0:T(8,128)(2,1)} %bitcast.34) | data formatting | bytes 8388608 | tf_op jit(solution)/shard_map/all_to_all | solution.py:28
  219.4 2.5 copy.49
  221.8 4.5 copy.51
  226.3 62.3 %all-to-all-done.1 = bf16[128,2,6,2048]{3,1,2,0:T(2,128)(2,1)} async-done(((bf16[128,2,6,2048]{3,1,2,0:T(2,128)(2,1)}), bf16[128,2,6,2048]{3,1,2,0:T(2,128)(2,1)}, u32[]{:S(2)}, u32[]{:S(2)}) %all-to-all-start.1) | async-done | bytes 6291488 | tf_op jit(solution)/shard_map/all_to_all | solution.py:53
  288.6 9.4 %fusion.3 = f32[2,768,512]{2,1,0:T(8,128)} fusion(bf16[2,2048,512]{2,1,0:T(8,128)(2,1)} %bitcast.36, bf16[2,768,2048]{2,0,1:T(2,128)(2,1)} %bitcast.8), kind=kOutput, calls=%fused_computation.14 | convolution fusion | flops 3221225472 | bytes 13631488 | tf_op jit(solution)/shard_map/scd,sdh->sch/dot_general | solution.py:72
  298.0 16.5 %fusion = bf16[1,2,768,2048]{3,2,1,0:T(8,128)(2,1)} fusion(pred[2,768]{1,0:T(4,128)(4,1)S(1)} %compare_and_fusion, bf16[2,2048,512]{2,1,0:T(8,128)(2,1)} %bitcast.40, f32[2,768,512]{2,1,0:T(8,128)} %fusion.3, bf16[2,2048,512]{2,1,0:T(8,128)(2,1)} %bitcast.38, bf16[2,768,2048]{2,0,1:T(2,128)(2,1)} %bitcast.8), kind=kOutput, calls=%fused_computation.11 | convolution fusion | flops 6453460992 | bytes 24118784 | tf_op jit(solution)/shard_map/sch,sdh->scd/dot_general | solution.py:77
  314.4 12.6 %copy.52 = bf16[1,2,768,2048]{3,1,0,2:T(2,128)(2,1)} copy(bf16[1,2,768,2048]{3,2,1,0:T(8,128)(2,1)} %fusion) | data formatting | bytes 12582912 | tf_op jit(solution)/shard_map/reshape | solution.py:79
  327.1 6.0 %all-to-all-start.5 = ((bf16[1,2,768,2048]{3,1,0,2:T(2,128)(2,1)}), bf16[1,2,768,2048]{3,1,0,2:T(2,128)(2,1)}, u32[]{:S(2)}, u32[]{:S(2)}) async-start(bf16[1,2,768,2048]{3,1,0,2:T(2,128)(2,1)} %copy.52), calls=%async_computation.5 | async-start | bytes 12582912 | tf_op jit(solution)/shard_map/all_to_all | solution.py:80
  333.1 0.1 copy.42
  333.3 0.1 copy.41
  333.5 74.9 %all-to-all-done.5 = bf16[1,2,768,2048]{3,1,0,2:T(2,128)(2,1)} async-done(((bf16[1,2,768,2048]{3,1,0,2:T(2,128)(2,1)}), bf16[1,2,768,2048]{3,1,0,2:T(2,128)(2,1)}, u32[]{:S(2)}, u32[]{:S(2)}) %all-to-all-start.5) | async-done | bytes 6291488 | tf_op jit(solution)/shard_map/all_to_all | solution.py:80
  408.3 10.4 %copy.53 = bf16[128,1,2,6,2048]{4,3,2,0,1:T(8,128)(2,1)} copy(bf16[128,1,2,6,2048]{4,2,3,0,1:T(2,128)(2,1)} %bitcast.22) | data formatting | bytes 12582912 | tf_op jit(solution)/shard_map/all_to_all | solution.py:80
  418.7 11.1 %reshape.178 = bf16[1536,2048]{1,0:T(8,128)(2,1)} reshape(bf16[128,1,2,6,2048]{4,3,2,0,1:T(8,128)(2,1)} %copy.53) | data formatting | bytes 12582912 | tf_op jit(solution)/shard_map/reshape | solution.py:83
  429.8 14.4 %gather_fusion.1 = bf16[1280,2048]{1,0:T(8,128)(2,1)} fusion(bf16[1536,2048]{1,0:T(8,128)(2,1)} %reshape.178, s32[2048]{0:T(1024)S(1)} %pad_clamp_fusion), kind=kCustom, calls=%fused_computation.4 | custom fusion | bytes 10490880 | tf_op jit(solution)/shard_map/jit(_take)/gather | solution.py:84
  444.2 9.6 %gather.18 = bf16[128,10,2048]{2,1,0:T(8,128)(2,1)} reshape(bf16[1280,2048]{1,0:T(8,128)(2,1)} %gather_fusion.1) | data formatting | bytes 10485760 | tf_op jit(solution)/shard_map/jit(_take)/gather | solution.py:84
  453.8 9.7 %multiply_reduce_fusion = bf16[128,2048]{1,0:T(8,128)(2,1)} fusion(bf16[128,10,2048]{2,1,0:T(8,128)(2,1)} %gather.18, f32[128,10]{1,0:T(8,128)S(1)} %copy.41, pred[128,10]{1,0:T(8,128)(4,1)S(1)} %copy.42), kind=kLoop, calls=%fused_computation.8 | loop fusion | flops 10223616 | bytes 5773568 | tf_op jit(solution)/shard_map/reduce_sum | solution.py:86
  (38 shorter events, 0.7 us)
Async XLA Ops:
  0.6 159.3 %copy-start = (bf16[128,2048]{1,0:T(8,128)(2,1)S(1)}, bf16[128,2048]{1,0:T(8,128)(2,1)}, u32[]{:S(2)}) copy-start(bf16[128,2048]{1,0:T(8,128)(2,1)} %param.10) | copy-start | bytes 1572868
  6.2 36.4 %all-to-all-start = ((s32[128,2,1]{1,2,0:T(1,128)}), s32[128,2,1]{1,2,0:T(1,128)S(1)}, u32[]{:S(2)}, u32[]{:S(2)}) async-start(s32[128,2,1]{1,2,0:T(1,128)} %bitcast), calls=%async_computation | async-start | bytes 131072 | tf_op jit(solution)/shard_map/all_to_all | solution.py:54
  42.6 54.2 %copy-start.3 = (bf16[8,512,512]{2,1,0:T(8,128)(2,1)S(1)}, bf16[8,512,512]{2,1,0:T(8,128)(2,1)}, u32[]{:S(2)}) copy-start(bf16[8,512,512]{2,1,0:T(8,128)(2,1)} %get-tuple-element.12) | copy-start | bytes 12582916
  148.4 55.3 %all-to-all-start.4 = ((bf16[8,512,512]{2,1,0:T(8,128)(2,1)}), bf16[8,512,512]{2,1,0:T(8,128)(2,1)}, u32[]{:S(2)}, u32[]{:S(2)}) async-start(bf16[8,512,512]{2,1,0:T(8,128)(2,1)} %get-tuple-element.13), calls=%async_computation.4 | async-start | bytes 8388608 | tf_op jit(solution)/shard_map/all_to_all | solution.py:30
  203.7 9.9 %copy-start.5 = (s32[256]{0:T(256)S(1)}, s32[256]{0:T(256)}, u32[]{:S(2)}) copy-start(s32[256]{0:T(256)} %param.14) | copy-start | bytes 3076
  203.7 84.9 %all-to-all-start.1 = ((bf16[128,2,6,2048]{3,1,2,0:T(2,128)(2,1)}), bf16[128,2,6,2048]{3,1,2,0:T(2,128)(2,1)}, u32[]{:S(2)}, u32[]{:S(2)}) async-start(bf16[128,2,6,2048]{3,1,2,0:T(2,128)(2,1)} %copy.46), calls=%async_computation.1 | async-start | bytes 12582912 | tf_op jit(solution)/shard_map/all_to_all | solution.py:53
  214.7 4.6 %copy-start.2 = (bf16[8,512,512]{2,1,0:T(8,128)(2,1)S(1)}, bf16[8,512,512]{2,1,0:T(8,128)(2,1)}, u32[]{:S(2)}) copy-start(bf16[8,512,512]{2,1,0:T(8,128)(2,1)} %all_to_all.100) | copy-start | bytes 12582916
  327.1 6.2 %copy-start.4 = (f32[128,10]{0,1:T(8,128)S(1)}, f32[128,10]{0,1:T(8,128)}, u32[]{:S(2)}) copy-start(f32[128,10]{0,1:T(8,128)} %param.12) | copy-start | bytes 15364
  327.1 81.3 %all-to-all-start.5 = ((bf16[1,2,768,2048]{3,1,0,2:T(2,128)(2,1)}), bf16[1,2,768,2048]{3,1,0,2:T(2,128)(2,1)}, u32[]{:S(2)}, u32[]{:S(2)}) async-start(bf16[1,2,768,2048]{3,1,0,2:T(2,128)(2,1)} %copy.52), calls=%async_computation.5 | async-start | bytes 12582912 | tf_op jit(solution)/shard_map/all_to_all | solution.py:80
  444.2 19.3 %copy-start.1 = (bf16[128,2048]{1,0:T(8,128)(2,1)S(1)}, bf16[128,2048]{1,0:T(8,128)(2,1)}, u32[]{:S(2)}) copy-start(bf16[128,2048]{1,0:T(8,128)(2,1)} %param.10) | copy-start | bytes 1572868
where the time goes:
time: 465 us; the launch traced here: 464 us
  waiting for transfers between devices  137 us (29%)
  local copies, waits for them, and re-layouts  133 us (29%)
  blocking collectives  106 us (23%)
  starting transfers between devices  33.1 us (7%)
  other arithmetic  27.6 us (6%)
  matrix products  25.9 us (6%)
    all_to_all x1, waiting for transfers between devices, local(): lax.all_to_all(joint_result, ('expert', 'replica'), split_axis=2, concat_...  74.9 us
    all_to_all x1, waiting for transfers between devices, local(): lax.all_to_all(joint_rows, ('expert', 'replica'), split_axis=0, concat_ax...  62.3 us
    all_to_all x1, blocking collectives, local(): lax.all_to_all(ordered[0], 'replica', split_axis=0, concat_axis=1, tiled=...  54.2 us
    all_to_all x1, blocking collectives, local(): lax.all_to_all(ordered[1], 'replica', split_axis=0, concat_axis=1, tiled=...  51.6 us
    gather x2, local copies, waits for them, and re-layouts, local(): jnp.take(returned, flat_index, axis=0).reshape(tok_count, top_count, width)  24 us
    gather x2, local copies, waits for them, and re-layouts, local(): jnp.take(tokens, row_source, axis=0)  18 us
    dot_general x1, matrix products, local(): jnp.einsum('sch,sdh->scd', hidden, rollout[2], preferred_element_type=jnp...  16.5 us
    select_n x1, local copies, waits for them, and re-layouts, local(): jnp.where(filled[:, None] > 0, jnp.take(tokens, row_source, axis=0), jnp....  15.2 us
  transfers between devices with their start and end apart: 4, of which 2 were waited for; matrix products, arithmetic and copies ran while one was open for 19% of the time, Pallas kernels for 0%

commit v1 on v0

v1 whole, which is shorter than its diff:
```python
import jax
import jax.numpy as jnp
from jax import lax
from jax.experimental import pallas as pl
from jax.experimental.pallas import tpu as pltpu
from jax.sharding import PartitionSpec as P

MESH = pl.DeviceIdType.MESH
BF = jnp.bfloat16
F32 = jnp.float32
ROWS = 48
PEERS = 16
ALL = ROWS * PEERS
D = 2048
H = 512


def kernel(
    tok, ids, scores, lane, cap, tg, tu, td,
    comb, og, ou, od,
    big, stage, wbuf, xall, send, recv, pmat, wmat, hid, idr, bout, binr,
    meta, mask3, key3, gate3, cnt, tmp,
    s_t, s_x, r_x, s_meta, r_meta, s_w, r_w, l_w, s_cnt, r_cnt, s_d, r_d,
    s_ret, r_ret, s_sib, r_sib, s_idle, r_idle, s_busy, r_busy, l_x, l_in,
):
    e = lax.axis_index("expert")
    r = lax.axis_index("replica")
    g, xh = e // 2, e % 2
    xl, c = r // 2, r % 2
    z, y = g // 4, g % 4
    o = xh * 4 + r
    tgt = (r, r + 1 - 2 * c, (r + 2) % 4, 3 - r)
    e_far = e + 1 - 2 * xh
    train, outs = (tg, tu, td), (og, ou, od)

    def dev(ee, rr):
        return {"expert": ee, "replica": rr}

    def plane(dz, dy):
        return dev((((z + dz + 4) % 4) * 4 + (y + dy + 4) % 4) * 2 + xh, r)

    def remote(src, dst, ssem, rsem, device):
        return pltpu.make_async_remote_copy(
            src_ref=src, dst_ref=dst, send_sem=ssem, recv_sem=rsem, device_id=device, device_id_type=MESH
        )

    def wait(ref, sem):
        pltpu.make_async_copy(ref, ref, sem).wait()

    loads = [pltpu.make_async_copy(train[w], big.at[pl.ds(w * 4096, 4096)], s_t.at[w]) for w in range(3)]
    for copy in loads:
        copy.start()
    tmp[...] = jnp.full((128, 128), -1.0, F32)
    tmp[:, 0:10] = ids[...].astype(F32)
    meta[o, 0:16, :] = jnp.transpose(tmp[...])[0:16]
    raw = scores[...]
    grown = jnp.exp(raw - jnp.max(raw, axis=1, keepdims=True))
    tmp[:, 0:10] = grown / jnp.sum(grown, axis=1, keepdims=True)
    meta[o, 16:32, :] = jnp.transpose(tmp[...])[0:16]

    barrier = pltpu.get_barrier_semaphore()
    group = [dev(e if f < 4 else e_far, tgt[f % 4]) for f in range(1, 8)]
    for device in group:
        pl.semaphore_signal(barrier, inc=1, device_id=device, device_id_type=MESH)

    def greet(m, _):
        pl.semaphore_signal(barrier, inc=1, device_id=plane(m // 4, m % 4), device_id_type=MESH)
        return 0

    lax.fori_loop(1, PEERS, greet, 0)
    pl.semaphore_wait(barrier, 7 + PEERS - 1)

    def block(b):
        return xall.at[pl.ds(pl.multiple_of(b * 128, 128), 128)]

    sib, busy, idle = dev(e, tgt[1]), dev(e, tgt[2]), dev(e_far, tgt[2])
    x_sends = [
        remote(tok, block(o), s_x.at[0], r_x.at[o], busy),
        remote(tok, block(o), s_x.at[1], r_x.at[o], idle),
        remote(tok, block(o), s_x.at[2], r_x.at[o], sib),
    ]
    for copy in x_sends:
        copy.start()
    own_x = pltpu.make_async_copy(tok, block(o), l_x)
    own_x.start()
    for device in group:
        remote(meta.at[o], meta.at[o], s_meta, r_meta, device).start()

    def find(column, k, table=None):
        at = jnp.int32(0)
        for j in range(8):
            at = at + jnp.where(lane[column * 8 + j] == k, j if table is None else table[column * 8 + j], 0)
        return at

    lanes = [lane[e * 8 + j] for j in range(8)]
    own_w = {}
    for i in range(2):
        for w in range(3):
            if i == 0:
                loads[w].wait()
            for k in (2, 3, 1, 0):
                n = (i * 3 + w) * 4 + k

                def choose(t, _):
                    at = pl.multiple_of(t * 64, 64)
                    kept = big[pl.ds(pl.multiple_of(w * 4096 + at, 64), 64), :]
                    for j in range(1, 8):
                        other = big[pl.ds(pl.multiple_of((w * 8 + j) * 512 + at, 64), 64), :]
                        kept = lax.select(lanes[j] == 2 * tgt[k] + i, other, kept)
                    stage[n, pl.ds(at, 64), :] = kept
                    return 0

                lax.fori_loop(0, 8, choose, 0)
                place = outs[w].at[i, pl.ds(pl.multiple_of(r * 512, 512), 512)]
                if k:
                    remote(stage.at[n], place, s_w, r_w.at[i, w, k], dev(e, tgt[k])).start()
                else:
                    own_w[i, w] = pltpu.make_async_copy(stage.at[n], place, l_w.at[i, w])
                    own_w[i, w].start()

    wait(meta.at[0:7], r_meta)
    named = [meta[:, k, :] for k in range(10)]
    gates = [meta[:, 16 + k, :] for k in range(10)]

    def expert_of(s):
        column = (s // 2) * 2 + xh
        return column * 8 + find(column, 2 * r + s % 2)

    def one_slot(s, _):
        expert = expert_of(s).astype(F32)
        hits = jnp.zeros((8, 128), F32)
        gate = jnp.zeros((8, 128), F32)
        for k in range(10):
            same = named[k] == expert
            hits = hits + jnp.where(same, 1.0, 0.0)
            gate = gate + jnp.where(same, gates[k], 0.0)
        mask3[s] = hits
        gate3[s] = gate
        return 0

    lax.fori_loop(0, 32, one_slot, 0)
    hits = mask3[...].reshape(256, 128)
    hits16 = hits.astype(BF)
    row = lax.broadcasted_iota(jnp.int32, (256, 256), 0)
    col = lax.broadcasted_iota(jnp.int32, (256, 256), 1)
    slot_same = (row >> 3) == (col >> 3)
    earlier_block = jnp.where(slot_same & (col < row), 1.0, 0.0).astype(BF)
    any_block = jnp.where(slot_same, 1.0, 0.0).astype(BF)
    earlier_token = jnp.where(row[0:128, 0:128] < col[0:128, 0:128], 1.0, 0.0).astype(BF)
    ones = jnp.ones((128, 128), BF)

    def mm(a, b):
        return jnp.dot(a, b, preferred_element_type=F32)

    rank = mm(hits16, earlier_token) + mm(mm(earlier_block, hits16).astype(BF), ones)
    key3[...] = jnp.where(hits > 0.5, rank, -1.0).reshape(32, 8, 128)
    mask3[...] = mm(mm(any_block, hits16).astype(BF), ones).reshape(32, 8, 128)
    cnt[g] = mask3[:, 0, :]

    def tell(m, _):
        remote(cnt.at[g], cnt.at[g], s_cnt, r_cnt, plane(m // 4, m % 4)).start()
        return 0

    lax.fori_loop(1, PEERS, tell, 0)

    ob, oi, oa = xh * 4 + tgt[2], (1 - xh) * 4 + tgt[2], (1 - xh) * 4 + r
    wait(block(ob), r_x.at[ob])
    x_sends.append(remote(block(ob), block(ob), s_x.at[3], r_x.at[ob], idle))
    x_sends.append(remote(block(ob), block(ob), s_x.at[4], r_x.at[ob], sib))
    x_sends[3].start()
    x_sends[4].start()
    wait(block(oi), r_x.at[oi])
    x_sends.append(remote(block(oi), block(oi), s_x.at[5], r_x.at[oi], sib))
    x_sends[5].start()
    wait(block(oa), r_x.at[oa])
    x_sends.append(remote(block(oa), block(oa), s_x.at[6], r_x.at[oa], sib))
    x_sends[6].start()
    own_x.wait()
    for b in (xh * 4 + tgt[1], xh * 4 + tgt[3], (1 - xh) * 4 + tgt[1], (1 - xh) * 4 + tgt[3]):
        wait(block(b), r_x.at[b])

    place48 = lax.broadcasted_iota(jnp.int32, (ROWS, 128), 0).astype(F32)

    def slot_at(m, i):
        dz, dy = m // 4, m % 4
        return (((z + dz) % 4) * 4 + (y + dy) % 4) * 2 + i

    place16 = place48[0:16]
    for i in range(2):
        for p in range(3):
            piece = i * 3 + p

            def pick(m, _):
                at = key3[slot_at(m, i)] - 16.0 * p
                for b in range(8):
                    pmat[pl.ds(pl.multiple_of(m * 16, 16), 16), b * 128 : b * 128 + 128] = jnp.where(
                        at[b : b + 1, :] == place16, 1.0, 0.0
                    ).astype(BF)
                return 0

            lax.fori_loop(0, PEERS, pick, 0)

            def gather(n, _):
                cols = pl.ds(pl.multiple_of(n * 512, 512), 512)
                send[piece, :, cols] = mm(pmat[0:256, :], xall[:, cols]).astype(BF)
                return 0

            lax.fori_loop(0, 4, gather, 0)

            def dispatch(m, _):
                src = send.at[piece, pl.ds(pl.multiple_of(m * 16, 16), 16)]
                dst = recv.at[i, pl.ds(pl.multiple_of(m * ROWS + p * 16, 16), 16)]
                remote(src, dst, s_d, r_d.at[i], plane(m // 4, m % 4)).start()
                return 0

            lax.fori_loop(1, PEERS, dispatch, 0)
            recv[i, p * 16 : p * 16 + 16, :] = send[piece, 0:16, :]

    wait(cnt.at[0:15], r_cnt)

    def before(p, total):
        return total + cnt[p] * jnp.where(p < g, 1.0, 0.0)

    seen = lax.fori_loop(0, PEERS, before, jnp.zeros((32, 128), F32))
    tmp[0:32, :] = seen

    def drop(s, _):
        room = find((s // 2) * 2 + xh, 2 * r + s % 2, cap).astype(F32) - tmp[pl.ds(s, 1), :]
        gate3[s] = jnp.where(key3[s] < room, gate3[s], 0.0)
        return 0

    lax.fori_loop(0, 32, drop, 0)

    def weigh(i, half):
        def fill(n, _):
            s = slot_at(half * 8 + n, i)
            at, gate = key3[s], gate3[s]
            for b in range(8):
                spot = (b % 2) * 4 + b // 2
                pmat[pl.ds(pl.multiple_of(n * ROWS, 16), ROWS), spot * 128 : spot * 128 + 128] = jnp.where(
                    at[b : b + 1, :] == place48, gate[b : b + 1, :], 0.0
                ).astype(BF)
            return 0

        lax.fori_loop(0, 8, fill, 0)
        wmat[i, :, half * 384 : half * 384 + 384] = jnp.transpose(pmat[...])

    for i in range(2):
        for half in range(2):
            weigh(i, half)

    def block_of(i, w, k):
        return outs[w].at[i, pl.ds(pl.multiple_of(tgt[k] * 512, 512), 512)]

    def arrived(i, w, k):
        if k:
            wait(block_of(i, w, k), r_w.at[i, w, k])
        else:
            own_w[i, w].wait()

    def hidden(i):
        wait(recv.at[i, 0:720], r_d.at[i])
        fetch = []
        for w in range(2):
            for k in range(4):
                arrived(i, w, k)
            fetch.append(pltpu.make_async_copy(outs[w].at[i], wbuf.at[w], l_in.at[w]))
            fetch[w].start()
        for copy in fetch:
            copy.wait()

        def part(n, _):
            cols = pl.ds(pl.multiple_of(n * 256, 256), 256)
            gate = mm(recv[i], wbuf[0, :, cols])
            up = mm(recv[i], wbuf[1, :, cols])
            hid[:, cols] = (gate / (1.0 + jnp.exp(-gate)) * up).astype(BF)
            return 0

        lax.fori_loop(0, 2, part, 0)

    def returned(i, k):
        return big.at[pl.ds((i * 4 + k) * ALL, ALL)]

    def produce(i, k):
        arrived(i, 2, k)
        here = wbuf.at[2, pl.ds(k * 512, 512)]
        fetch = pltpu.make_async_copy(block_of(i, 2, k), here, l_in.at[2])
        fetch.start()
        fetch.wait()
        for n in range(2):
            at = k * 512 + n * 256
            recv[i, :, at : at + 256] = lax.dot_general(
                hid[...], wbuf[2, at : at + 256, :], (((1,), (1,)), ((), ())), preferred_element_type=F32
            ).astype(BF)

        def give_back(m, _):
            src = recv.at[i, pl.ds(pl.multiple_of(m * ROWS, 16), ROWS), pl.ds(k * 512, 512)]
            dst = big.at[pl.ds(pl.multiple_of((i * 4 + k) * ALL + m * ROWS, 16), ROWS)]
            remote(src, dst, s_ret, r_ret.at[i, k], plane(-(m // 4), -(m % 4))).start()
            return 0

        lax.fori_loop(1, PEERS, give_back, 0)
        big[(i * 4 + k) * ALL : (i * 4 + k) * ALL + ROWS, :] = recv[i, 0:ROWS, k * 512 : k * 512 + 512]

    def partial(k):
        return 6144 + k * 1024

    def sibling(k):
        return 10240 + k * 512

    tail = []

    def combine(k):
        for i in range(2):
            base = (i * 4 + k) * ALL
            wait(big.at[pl.ds(base, 720)], r_ret.at[i, k])
        for n in range(2):
            cols = slice(n * 256, n * 256 + 256)
            total = mm(wmat[0], big[k * ALL : k * ALL + ALL, cols])
            total = total + mm(wmat[1], big[(4 + k) * ALL : (4 + k) * ALL + ALL, cols])
            big[partial(k) : partial(k) + 1024, cols] = total.astype(BF)
        k2 = k ^ 1
        tail.append(
            remote(
                big.at[pl.ds(pl.multiple_of(partial(k) + (1 - c) * 512, 512), 512)],
                big.at[pl.ds(sibling(k2), 512)],
                s_sib.at[k], r_sib.at[k2], sib,
            )
        )
        tail[-1].start()

    def own(k):
        return pl.multiple_of(partial(k) + c * 512, 512)

    def to_idle(k):
        wait(big.at[pl.ds(sibling(k), 512)], r_sib.at[k])
        both = big[pl.ds(own(k), 512), :].astype(F32) + big[sibling(k) : sibling(k) + 512, :].astype(F32)
        big[pl.ds(own(k), 512), :] = both.astype(BF)
        k2 = k ^ 2
        tail.append(
            remote(
                big.at[pl.ds(pl.multiple_of(own(k) + (1 - xh) * 256, 256), 256)],
                idr.at[k2], s_idle.at[k], r_idle.at[k2], idle,
            )
        )
        tail[-1].start()

    def to_busy(k):
        wait(idr.at[k], r_idle.at[k])
        there = pl.multiple_of((1 - xl) * 128, 128)
        mine = big[pl.ds(pl.multiple_of(own(k) + xh * 256 + (1 - xl) * 128, 128), 128), :].astype(F32)
        bout[k] = (mine + idr[k, pl.ds(there, 128), :].astype(F32)).astype(BF)
        k2 = k ^ 2
        tail.append(remote(bout.at[k], binr.at[k2], s_busy.at[k], r_busy.at[k2], busy))
        tail[-1].start()

    def finish(k):
        wait(binr.at[k], r_busy.at[k])
        here = pl.multiple_of(xl * 128, 128)
        mine = big[pl.ds(pl.multiple_of(own(k) + xh * 256 + xl * 128, 128), 128), :].astype(F32)
        total = mine + idr[k, pl.ds(here, 128), :].astype(F32) + binr[k].astype(F32)
        comb[:, pl.ds(pl.multiple_of(tgt[k] * 512, 512), 512)] = total.astype(BF)

    hidden(0)
    for k in range(4):
        produce(0, k)
    hidden(1)
    produce(1, 0)
    produce(1, 1)
    produce(1, 2)
    combine(0)
    combine(1)
    produce(1, 3)
    to_idle(0)
    to_idle(1)
    combine(2)
    combine(3)
    to_idle(2)
    to_idle(3)
    to_busy(2)
    to_busy(3)
    to_busy(0)
    to_busy(1)
    for k in (2, 3, 0, 1):
        finish(k)

    for copy in x_sends + tail:
        copy.wait_send()
    wait(meta.at[0:7], s_meta)
    wait(stage.at[0:18], s_w)
    wait(cnt.at[0:15], s_cnt)
    wait(recv.at[:, 0:720], s_d)
    wait(recv.at[:, 0:720], s_ret)


def local(tokens, expert_ids, router_scores, lane_list, capacity, train_gate, train_up, train_down):
    dma = pltpu.SemaphoreType.DMA
    out_w = jax.ShapeDtypeStruct((2, D, H), BF)
    anywhere = pl.BlockSpec(memory_space=pl.ANY)
    vmem = pl.BlockSpec(memory_space=pltpu.VMEM)
    smem = pl.BlockSpec(memory_space=pltpu.SMEM)
    return pl.pallas_call(
        kernel,
        out_shape=(jax.ShapeDtypeStruct((128, D), BF), out_w, out_w, out_w),
        in_specs=[anywhere, vmem, vmem, smem, smem, anywhere, anywhere, anywhere],
        out_specs=[vmem, anywhere, anywhere, anywhere],
        scratch_shapes=[
            pltpu.VMEM((12288, 512), BF),
            pltpu.VMEM((24, 512, 512), BF),
            pltpu.VMEM((3, D, H), BF),
            pltpu.VMEM((1024, D), BF),
            pltpu.VMEM((6, 256, D), BF),
            pltpu.VMEM((2, ALL, D), BF),
            pltpu.VMEM((384, 1024), BF),
            pltpu.VMEM((2, 1024, ALL), BF),
            pltpu.VMEM((ALL, H), BF),
            pltpu.VMEM((4, 256, 512), BF),
            pltpu.VMEM((4, 128, 512), BF),
            pltpu.VMEM((4, 128, 512), BF),
            pltpu.VMEM((8, 32, 128), F32),
            pltpu.VMEM((32, 8, 128), F32),
            pltpu.VMEM((32, 8, 128), F32),
            pltpu.VMEM((32, 8, 128), F32),
            pltpu.VMEM((16, 32, 128), F32),
            pltpu.VMEM((128, 128), F32),
            dma((3,)), dma((7,)), dma((8,)), dma, dma, dma, dma((2, 3, 4)), dma((2, 3)), dma, dma,
            dma, dma((2,)), dma, dma((2, 4)),
            dma((4,)), dma((4,)), dma((4,)), dma((4,)), dma((4,)), dma((4,)), dma, dma((3,)),
        ],
        compiler_params=pltpu.CompilerParams(
            collective_id=0, has_side_effects=True, vmem_limit_bytes=63 << 20
        ),
        name="resync_moe",
    )(
        tokens, expert_ids, router_scores, lane_list, capacity,
        train_gate.reshape(4096, 512), train_up.reshape(4096, 512), train_down.reshape(4096, 512),
    )


def solution(mesh):
    both = ("expert", "replica")
    return jax.shard_map(
        local,
        mesh=mesh,
        in_specs=(
            P(both, None), P(both, None), P(both, None), P(), P(),
            P("expert", "replica", None), P("expert", "replica", None), P("expert", "replica", None),
        ),
        out_specs=(P(both, None), P(both, None, None), P(both, None, None), P(both, None, None)),
        check_vma=False,
    )
```

time: 465 us -> 237 us (0.51)
  Pallas kernels: 0 us -> 220 us
  waiting for transfers between devices: 137 us -> 0 us
  local copies, waits for them, and re-layouts: 133 us -> 15.1 us
  blocking collectives: 106 us -> 0 us
  starting transfers between devices: 33.1 us -> 0 us
  other arithmetic: 27.6 us -> 0 us
  matrix products: 25.9 us -> 0 us
    pallas_call x0 -> x1, Pallas kernels: none -> 220 us  [local(): pl.pallas_call(kernel, out_shape=(jax.ShapeDtypeStruct((128, D), BF), out...]
    all_to_all x4 -> x0, waiting for transfers between devices: 137 us -> none  [the longest x1 74.9 us: local(): lax.all_to_all(joint_result, ('expert', 'replica'), split_axis=2, concat_...]
    all_to_all x2 -> x0, blocking collectives: 106 us -> none  [the longest x1 54.2 us: local(): lax.all_to_all(ordered[0], 'replica', split_axis=0, concat_axis=1, tiled=...]
    gather x7 -> x0, local copies, waits for them, and re-layouts: 57.1 us -> none  [the longest x2 24 us: local(): jnp.take(returned, flat_index, axis=0).reshape(tok_count, top_count, width)]
    all_to_all x4 -> x0, starting transfers between devices: 33.1 us -> none  [the longest x1 11.5 us: local(): lax.all_to_all(joint_counts, ('expert', 'replica'), split_axis=0, concat_...]
    dot_general x2 -> x0, matrix products: 25.9 us -> none  [the longest x1 16.5 us: local(): jnp.einsum('sch,sdh->scd', hidden, rollout[2], preferred_element_type=jnp...]
    reshape x4 -> x0, local copies, waits for them, and re-layouts: 24.6 us -> none  [the longest x1 12.6 us: local(): joint_result = result.reshape(1, per_device, device_count * slot_cap, width)]
    all_to_all x5 -> x0, local copies, waits for them, and re-layouts: 22 us -> none  [the longest x1 10.4 us: local(): lax.all_to_all(joint_result, ('expert', 'replica'), split_axis=2, concat_...]
  transfers between devices with their start and end apart: 4 -> 0, of which waited for: 2 -> 0; matrix products, arithmetic and copies ran while one was open for 19% -> 0% of each run, Pallas kernels for 0% -> 0%
where the time goes in v1:
time: 237 us; the launch traced here: 236 us
  Pallas kernels  220 us (93%)
  local copies, waits for them, and re-layouts  15.1 us (6%)
    pallas_call x1, Pallas kernels, local(): pl.pallas_call(kernel, out_shape=(jax.ShapeDtypeStruct((128, D), BF), out...  220 us
    unnamed x10, local copies, waits for them, and re-layouts  15.1 us

profile of v1, /device:TPU:1, one launch (start us, length us, event | category | flops | bytes accessed | tf_op | source)
XLA Modules:
  0.0 235.6 jit_solution(18060096374306051606)
XLA Ops:
  0.6 1.4 copy.12.ids
  2.1 1.4 copy.13.scores
  3.5 219.8 %resync_moe.1 = (bf16[128,2048]{1,0:T(8,128)(2,1)}, bf16[2,2048,512]{2,1,0:T(8,128)(2,1)}, bf16[2,2048,512]{2,1,0:T(8,128)(2,1)}, bf16[2,2048,512]{2,1,0:T(8,128)(2,1)}) custom-call(bf16[128,2048]{1,0:T(8,128)(2,1)} %tok.1, s32[128,10]{1,0:T(8,128)} %copy.12.ids, f32[128,10]{1,0:T(8,128)} %copy.13.scores, s32[256]{0:T(256)} %lane.1, s32[256]{0:T(256)} %cap.1, ...), custom_call_target="tpu_custom_call" | custom-call | tf_op jit(solution)/shard_map/resync_moe/pallas_call | solution.py:402
  223.3 1.9 copy.18
  225.2 0.0 copy-start.1
  225.2 4.6 %copy.19 = bf16[2,2048,512]{2,1,0:T(8,128)(2,1)} copy(bf16[2,2048,512]{2,1,0:T(8,128)(2,1)} %get-tuple-element.9) | data formatting | bytes 8388608
  229.9 0.0 copy-done.1
  229.9 0.0 copy-start
  229.9 2.1 copy.20
  232.0 1.6 copy-done
  233.6 2.0 copy.21
Async XLA Ops:
  225.2 4.6 %copy-start.1 = (bf16[2,2048,512]{2,1,0:T(8,128)(2,1)S(1)}, bf16[2,2048,512]{2,1,0:T(8,128)(2,1)}, u32[]{:S(2)}) copy-start(bf16[2,2048,512]{2,1,0:T(8,128)(2,1)} %get-tuple-element.10) | copy-start | bytes 12582916
  229.9 3.7 %copy-start = (bf16[2,2048,512]{2,1,0:T(8,128)(2,1)S(1)}, bf16[2,2048,512]{2,1,0:T(8,128)(2,1)}, u32[]{:S(2)}) copy-start(bf16[2,2048,512]{2,1,0:T(8,128)(2,1)} %get-tuple-element.11) | copy-start | bytes 12582916

commit v2 on v1

--- a/solution.py
+++ b/solution.py
@@ -19,8 +19,8 @@
     tok, ids, scores, lane, cap, tg, tu, td,
     comb, og, ou, od,
     big, stage, wbuf, xall, send, recv, pmat, wmat, hid, idr, bout, binr,
-    meta, mask3, key3, gate3, cnt, tmp,
-    s_t, s_x, r_x, s_meta, r_meta, s_w, r_w, l_w, s_cnt, r_cnt, s_d, r_d,
+    meta, mask3, key3, row3, gate3, cnt, tmp,
+    s_t, s_x, r_x, s_meta, r_meta, s_w, r_w, s_cnt, r_cnt, s_d, r_d,
     s_ret, r_ret, s_sib, r_sib, s_idle, r_idle, s_busy, r_busy, l_x, l_in,
 ):
     e = lax.axis_index("expert")
@@ -50,13 +50,10 @@
     loads = [pltpu.make_async_copy(train[w], big.at[pl.ds(w * 4096, 4096)], s_t.at[w]) for w in range(3)]
     for copy in loads:
         copy.start()
-    tmp[...] = jnp.full((128, 128), -1.0, F32)
-    tmp[:, 0:10] = ids[...].astype(F32)
-    meta[o, 0:16, :] = jnp.transpose(tmp[...])[0:16]
+    meta[o, 0:10, :] = ids[...].astype(F32)
     raw = scores[...]
-    grown = jnp.exp(raw - jnp.max(raw, axis=1, keepdims=True))
-    tmp[:, 0:10] = grown / jnp.sum(grown, axis=1, keepdims=True)
-    meta[o, 16:32, :] = jnp.transpose(tmp[...])[0:16]
+    grown = jnp.exp(raw - jnp.max(raw, axis=0, keepdims=True))
+    meta[o, 16:26, :] = grown / jnp.sum(grown, axis=0, keepdims=True)
 
     barrier = pltpu.get_barrier_semaphore()
     group = [dev(e if f < 4 else e_far, tgt[f % 4]) for f in range(1, 8)]
@@ -93,7 +90,6 @@
         return at
 
     lanes = [lane[e * 8 + j] for j in range(8)]
-    own_w = {}
     for i in range(2):
         for w in range(3):
             if i == 0:
@@ -113,10 +109,9 @@
                 lax.fori_loop(0, 8, choose, 0)
                 place = outs[w].at[i, pl.ds(pl.multiple_of(r * 512, 512), 512)]
                 if k:
-                    remote(stage.at[n], place, s_w, r_w.at[i, w, k], dev(e, tgt[k])).start()
+                    remote(stage.at[n], place, s_w, r_w.at[i, w, r], dev(e, tgt[k])).start()
                 else:
-                    own_w[i, w] = pltpu.make_async_copy(stage.at[n], place, l_w.at[i, w])
-                    own_w[i, w].start()
+                    pltpu.make_async_copy(stage.at[n], place, r_w.at[i, w, r]).start()
 
     wait(meta.at[0:7], r_meta)
     named = [meta[:, k, :] for k in range(10)]
@@ -145,6 +140,7 @@
     col = lax.broadcasted_iota(jnp.int32, (256, 256), 1)
     slot_same = (row >> 3) == (col >> 3)
     earlier_block = jnp.where(slot_same & (col < row), 1.0, 0.0).astype(BF)
+    earlier_half = jnp.where(((row >> 2) == (col >> 2)) & (col < row), 1.0, 0.0).astype(BF)
     any_block = jnp.where(slot_same, 1.0, 0.0).astype(BF)
     earlier_token = jnp.where(row[0:128, 0:128] < col[0:128, 0:128], 1.0, 0.0).astype(BF)
     ones = jnp.ones((128, 128), BF)
@@ -152,8 +148,13 @@
     def mm(a, b):
         return jnp.dot(a, b, preferred_element_type=F32)
 
-    rank = mm(hits16, earlier_token) + mm(mm(earlier_block, hits16).astype(BF), ones)
-    key3[...] = jnp.where(hits > 0.5, rank, -1.0).reshape(32, 8, 128)
+    within = mm(hits16, earlier_token)
+    rank = within + mm(mm(earlier_block, hits16).astype(BF), ones)
+    key3[...] = rank.reshape(32, 8, 128)
+    near = ((row[:, 0:128] >> 2) % 2) == xh
+    rank = within + mm(mm(earlier_half, hits16).astype(BF), ones)
+    at = jnp.where(near, jnp.where(rank < 16.0, rank, rank + 16.0), jnp.where(rank < 16.0, rank + 16.0, rank + 24.0))
+    row3[...] = jnp.where(hits > 0.5, at, -1.0).reshape(32, 8, 128)
     mask3[...] = mm(mm(any_block, hits16).astype(BF), ones).reshape(32, 8, 128)
     cnt[g] = mask3[:, 0, :]
 
@@ -163,58 +164,72 @@
 
     lax.fori_loop(1, PEERS, tell, 0)
 
+    def forward(b, n, device):
+        x_sends.append(remote(block(b), block(b), s_x.at[n], r_x.at[b], device))
+        x_sends[-1].start()
+
     ob, oi, oa = xh * 4 + tgt[2], (1 - xh) * 4 + tgt[2], (1 - xh) * 4 + r
     wait(block(ob), r_x.at[ob])
-    x_sends.append(remote(block(ob), block(ob), s_x.at[3], r_x.at[ob], idle))
-    x_sends.append(remote(block(ob), block(ob), s_x.at[4], r_x.at[ob], sib))
-    x_sends[3].start()
-    x_sends[4].start()
+    forward(ob, 3, sib)
+    forward(ob, 4, idle)
     wait(block(oi), r_x.at[oi])
-    x_sends.append(remote(block(oi), block(oi), s_x.at[5], r_x.at[oi], sib))
-    x_sends[5].start()
-    wait(block(oa), r_x.at[oa])
-    x_sends.append(remote(block(oa), block(oa), s_x.at[6], r_x.at[oa], sib))
-    x_sends[6].start()
-    own_x.wait()
-    for b in (xh * 4 + tgt[1], xh * 4 + tgt[3], (1 - xh) * 4 + tgt[1], (1 - xh) * 4 + tgt[3]):
-        wait(block(b), r_x.at[b])
+    forward(oi, 5, sib)
 
     place48 = lax.broadcasted_iota(jnp.int32, (ROWS, 128), 0).astype(F32)
+    place16 = place48[0:16]
+    upper = place16 < 8.0
+    place8 = jnp.where(upper, place16, place16 - 8.0)
 
     def slot_at(m, i):
         dz, dy = m // 4, m % 4
         return (((z + dz) % 4) * 4 + (y + dy) % 4) * 2 + i
 
-    place16 = place48[0:16]
-    for i in range(2):
-        for p in range(3):
-            piece = i * 3 + p
-
-            def pick(m, _):
-                at = key3[slot_at(m, i)] - 16.0 * p
-                for b in range(8):
-                    pmat[pl.ds(pl.multiple_of(m * 16, 16), 16), b * 128 : b * 128 + 128] = jnp.where(
-                        at[b : b + 1, :] == place16, 1.0, 0.0
-                    ).astype(BF)
-                return 0
-
-            lax.fori_loop(0, PEERS, pick, 0)
-
-            def gather(n, _):
-                cols = pl.ds(pl.multiple_of(n * 512, 512), 512)
-                send[piece, :, cols] = mm(pmat[0:256, :], xall[:, cols]).astype(BF)
-                return 0
-
-            lax.fori_loop(0, 4, gather, 0)
-
-            def dispatch(m, _):
-                src = send.at[piece, pl.ds(pl.multiple_of(m * 16, 16), 16)]
-                dst = recv.at[i, pl.ds(pl.multiple_of(m * ROWS + p * 16, 16), 16)]
-                remote(src, dst, s_d, r_d.at[i], plane(m // 4, m % 4)).start()
-                return 0
-
-            lax.fori_loop(1, PEERS, dispatch, 0)
-            recv[i, p * 16 : p * 16 + 16, :] = send[piece, 0:16, :]
+    def dispatch(late, part):
+        half = (1 - xh) if late else xh
+        piece = late * 3 + part
+
+        def pick(m, _):
+            for b in range(4):
+                here = pl.ds(half * 4 + b, 1)
+                if part < 2:
+                    chosen = row3[slot_at(m, part), here, :] == place16 + 16.0 * late
+                else:
+                    both = jnp.where(upper, row3[slot_at(m, 0), here, :], row3[slot_at(m, 1), here, :])
+                    chosen = both == place8 + (32.0 + 8.0 * late)
+                pmat[pl.ds(pl.multiple_of(m * 16, 16), 16), b * 128 : b * 128 + 128] = jnp.where(chosen, 1.0, 0.0).astype(BF)
+            return 0
+
+        lax.fori_loop(0, PEERS, pick, 0)
+
+        def gather(n, _):
+            cols = pl.ds(pl.multiple_of(n * 512, 512), 512)
+            rows = pl.ds(pl.multiple_of(half * 512, 512), 512)
+            send[piece, :, cols] = mm(pmat[0:256, 0:512], xall[rows, cols]).astype(BF)
+            return 0
+
+        lax.fori_loop(0, 4, gather, 0)
+        slot, base = (part, late * 16) if part < 2 else (late, 32)
+
+        def give(m, _):
+            src = send.at[piece, pl.ds(pl.multiple_of(m * 16, 16), 16)]
+            dst = recv.at[slot, pl.ds(pl.multiple_of(m * ROWS + base, 16), 16)]
+            remote(src, dst, s_d, r_d.at[part % 2], plane(m // 4, m % 4)).start()
+            return 0
+
+        lax.fori_loop(1, PEERS, give, 0)
+        recv[slot, base : base + 16, :] = send[piece, 0:16, :]
+
+    own_x.wait()
+    for b in (xh * 4 + tgt[1], xh * 4 + tgt[3]):
+        wait(block(b), r_x.at[b])
+    for part in (0, 2, 1):
+        dispatch(0, part)
+    wait(block(oa), r_x.at[oa])
+    forward(oa, 6, sib)
+    for b in ((1 - xh) * 4 + tgt[1], (1 - xh) * 4 + tgt[3]):
+        wait(block(b), r_x.at[b])
+    for part in (0, 2, 1):
+        dispatch(1, part)
 
     wait(cnt.at[0:15], r_cnt)
 
@@ -234,7 +249,7 @@
     def weigh(i, half):
         def fill(n, _):
             s = slot_at(half * 8 + n, i)
-            at, gate = key3[s], gate3[s]
+            at, gate = row3[s], gate3[s]
             for b in range(8):
                 spot = (b % 2) * 4 + b // 2
                 pmat[pl.ds(pl.multiple_of(n * ROWS, 16), ROWS), spot * 128 : spot * 128 + 128] = jnp.where(
@@ -249,17 +264,28 @@
         for half in range(2):
             weigh(i, half)
 
+    width = (xl * 2, xl * 2 + 1, (1 - xl) * 2, (1 - xl) * 2 + 1)
+
     def block_of(i, w, k):
-        return outs[w].at[i, pl.ds(pl.multiple_of(tgt[k] * 512, 512), 512)]
+        return outs[w].at[i, pl.ds(pl.multiple_of(width[k] * 512, 512), 512)]
 
     def arrived(i, w, k):
-        if k:
-            wait(block_of(i, w, k), r_w.at[i, w, k])
+        wait(block_of(i, w, k), r_w.at[i, w, width[k]])
+
+    def hidden(i):
+        if i == 0:
+            wait(recv.at[:, 0:480], r_d.at[0])
+
+            def sort(m, _):
+                rows = pl.ds(pl.multiple_of(m * ROWS + 32, 16), 16)
+                near, far = recv[0, rows, :].astype(F32), recv[1, rows, :].astype(F32)
+                recv[0, rows, :] = jnp.concatenate([near[0:8], far[0:8]], axis=0).astype(BF)
+                recv[1, rows, :] = jnp.concatenate([near[8:16], far[8:16]], axis=0).astype(BF)
+                return 0
+
+            lax.fori_loop(0, PEERS, sort, 0)
         else:
-            own_w[i, w].wait()
-
-    def hidden(i):
-        wait(recv.at[i, 0:720], r_d.at[i])
+            wait(recv.at[0, 0:480], r_d.at[1])
         fetch = []
         for w in range(2):
             for k in range(4):
@@ -319,7 +345,7 @@
             total = mm(wmat[0], big[k * ALL : k * ALL + ALL, cols])
             total = total + mm(wmat[1], big[(4 + k) * ALL : (4 + k) * ALL + ALL, cols])
             big[partial(k) : partial(k) + 1024, cols] = total.astype(BF)
-        k2 = k ^ 1
+        k2 = k
         tail.append(
             remote(
                 big.at[pl.ds(pl.multiple_of(partial(k) + (1 - c) * 512, 512), 512)],
@@ -359,29 +385,27 @@
         here = pl.multiple_of(xl * 128, 128)
         mine = big[pl.ds(pl.multiple_of(own(k) + xh * 256 + xl * 128, 128), 128), :].astype(F32)
         total = mine + idr[k, pl.ds(here, 128), :].astype(F32) + binr[k].astype(F32)
-        comb[:, pl.ds(pl.multiple_of(tgt[k] * 512, 512), 512)] = total.astype(BF)
+        comb[:, pl.ds(pl.multiple_of(width[k] * 512, 512), 512)] = total.astype(BF)
 
     hidden(0)
     for k in range(4):
         produce(0, k)
     hidden(1)
-    produce(1, 0)
-    produce(1, 1)
-    produce(1, 2)
+    for k in range(4):
+        produce(1, k)
     combine(0)
     combine(1)
-    produce(1, 3)
     to_idle(0)
     to_idle(1)
     combine(2)
+    to_idle(2)
+    to_busy(2)
     combine(3)
-    to_idle(2)
     to_idle(3)
-    to_busy(2)
     to_busy(3)
     to_busy(0)
     to_busy(1)
-    for k in (2, 3, 0, 1):
+    for k in range(4):
         finish(k)
 
     for copy in x_sends + tail:
@@ -421,9 +445,10 @@
             pltpu.VMEM((32, 8, 128), F32),
             pltpu.VMEM((32, 8, 128), F32),
             pltpu.VMEM((32, 8, 128), F32),
+            pltpu.VMEM((32, 8, 128), F32),
             pltpu.VMEM((16, 32, 128), F32),
             pltpu.VMEM((128, 128), F32),
-            dma((3,)), dma((7,)), dma((8,)), dma, dma, dma, dma((2, 3, 4)), dma((2, 3)), dma, dma,
+            dma((3,)), dma((7,)), dma((8,)), dma, dma, dma, dma((2, 3, 4)), dma, dma,
             dma, dma((2,)), dma, dma((2, 4)),
             dma((4,)), dma((4,)), dma((4,)), dma((4,)), dma((4,)), dma((4,)), dma, dma((3,)),
         ],
@@ -432,7 +457,7 @@
         ),
         name="resync_moe",
     )(
-        tokens, expert_ids, router_scores, lane_list, capacity,
+        tokens, expert_ids.T, router_scores.T, lane_list, capacity,
         train_gate.reshape(4096, 512), train_up.reshape(4096, 512), train_down.reshape(4096, 512),
     )
 

time: 237 us -> 212 us (0.89)
  Pallas kernels: 220 us -> 198 us
  local copies, waits for them, and re-layouts: 15.1 us -> 12.2 us
    pallas_call x1, Pallas kernels: 220 us -> 198 us  [local(): pl.pallas_call(kernel, out_shape=(jax.ShapeDtypeStruct((128, D), BF), out...]
    unnamed x10 -> x8, local copies, waits for them, and re-layouts: 15.1 us -> 12.2 us
where the time goes in v2:
time: 212 us; the launch traced here: 211 us
  Pallas kernels  198 us (93%)
  local copies, waits for them, and re-layouts  12.2 us (6%)
    pallas_call x1, Pallas kernels, local(): pl.pallas_call(kernel, out_shape=(jax.ShapeDtypeStruct((128, D), BF), out...  198 us
    unnamed x8, local copies, waits for them, and re-layouts  12.2 us

profile of v2, /device:TPU:1, one launch (start us, length us, event | category | flops | bytes accessed | tf_op | source)
XLA Modules:
  0.0 211.2 jit_solution(15616527411423375395)
XLA Ops:
  0.6 198.3 %resync_moe.1 = (bf16[128,2048]{1,0:T(8,128)(2,1)}, bf16[2,2048,512]{2,1,0:T(8,128)(2,1)}, bf16[2,2048,512]{2,1,0:T(8,128)(2,1)}, bf16[2,2048,512]{2,1,0:T(8,128)(2,1)}) custom-call(bf16[128,2048]{1,0:T(8,128)(2,1)} %tok.1, s32[10,128]{1,0:T(8,128)} %bitcast.8, f32[10,128]{1,0:T(8,128)} %bitcast.9, s32[256]{0:T(256)} %lane.1, s32[256]{0:T(256)} %cap.1, ...), custom_call_target="tpu_custom_call" | custom-call | tf_op jit(solution)/shard_map/resync_moe/pallas_call | solution.py:426
  199.0 1.9 copy.16
  200.8 0.0 copy-start.1
  200.8 4.6 %copy.17 = bf16[2,2048,512]{2,1,0:T(8,128)(2,1)} copy(bf16[2,2048,512]{2,1,0:T(8,128)(2,1)} %get-tuple-element.9) | data formatting | bytes 8388608
  205.5 0.0 copy-done.1
  205.5 0.0 copy-start
  205.5 2.1 %copy.18 = bf16[2,2048,512]{2,1,0:T(8,128)(2,1)} copy(bf16[2,2048,512]{2,1,0:T(8,128)(2,1)S(1)} %copy-done.1) | data formatting | bytes 8388608
  207.6 1.6 copy-done
  209.2 2.0 copy.19
Async XLA Ops:
  200.8 4.6 %copy-start.1 = (bf16[2,2048,512]{2,1,0:T(8,128)(2,1)S(1)}, bf16[2,2048,512]{2,1,0:T(8,128)(2,1)}, u32[]{:S(2)}) copy-start(bf16[2,2048,512]{2,1,0:T(8,128)(2,1)} %get-tuple-element.10) | copy-start | bytes 12582916
  205.5 3.7 %copy-start = (bf16[2,2048,512]{2,1,0:T(8,128)(2,1)S(1)}, bf16[2,2048,512]{2,1,0:T(8,128)(2,1)}, u32[]{:S(2)}) copy-start(bf16[2,2048,512]{2,1,0:T(8,128)(2,1)} %get-tuple-element.11) | copy-start | bytes 12582916

commit v3 on v2

--- a/solution.py
+++ b/solution.py
@@ -18,10 +18,10 @@
 def kernel(
     tok, ids, scores, lane, cap, tg, tu, td,
     comb, og, ou, od,
-    big, stage, wbuf, xall, send, recv, pmat, wmat, hid, idr, bout, binr,
+    big, stage, xall, send, recv, pmat, wmat, hid, idr, bout, binr,
     meta, mask3, key3, row3, gate3, cnt, tmp,
     s_t, s_x, r_x, s_meta, r_meta, s_w, r_w, s_cnt, r_cnt, s_d, r_d,
-    s_ret, r_ret, s_sib, r_sib, s_idle, r_idle, s_busy, r_busy, l_x, l_in,
+    s_ret, r_ret, s_sib, r_sib, s_idle, r_idle, s_busy, r_busy, l_x,
 ):
     e = lax.axis_index("expert")
     r = lax.axis_index("replica")
@@ -55,6 +55,36 @@
     grown = jnp.exp(raw - jnp.max(raw, axis=0, keepdims=True))
     meta[o, 16:26, :] = grown / jnp.sum(grown, axis=0, keepdims=True)
 
+    lanes = [lane[e * 8 + j] for j in range(8)]
+    tgts = (r, r + 1 - 2 * c, (1 - xl) * 2, (1 - xl) * 2 + 1)
+
+    def choose(i, w, k):
+        n = (i * 3 + w) * 4 + k
+
+        def some(t, _):
+            at = pl.multiple_of(t * 64, 64)
+            kept = big[pl.ds(pl.multiple_of(w * 4096 + at, 64), 64), :]
+            for j in range(1, 8):
+                other = big[pl.ds(pl.multiple_of((w * 8 + j) * 512 + at, 64), 64), :]
+                kept = lax.select(lanes[j] == 2 * tgts[k] + i, other, kept)
+            stage[n, pl.ds(at, 64), :] = kept
+            return 0
+
+        lax.fori_loop(0, 8, some, 0)
+
+    def post(i, w, k):
+        n = (i * 3 + w) * 4 + k
+        place = outs[w].at[i, pl.ds(pl.multiple_of(r * 512, 512), 512)]
+        if k:
+            remote(stage.at[n], place, s_w, r_w.at[i, w, r], dev(e, tgts[k])).start()
+        else:
+            pltpu.make_async_copy(stage.at[n], place, r_w.at[i, w, r]).start()
+
+    def ship(i, w, ks):
+        for k in ks:
+            choose(i, w, k)
+            post(i, w, k)
+
     barrier = pltpu.get_barrier_semaphore()
     group = [dev(e if f < 4 else e_far, tgt[f % 4]) for f in range(1, 8)]
     for device in group:
@@ -65,6 +95,9 @@
         return 0
 
     lax.fori_loop(1, PEERS, greet, 0)
+    loads[0].wait()
+    for k in (2, 3, 1, 0):
+        choose(0, 0, k)
     pl.semaphore_wait(barrier, 7 + PEERS - 1)
 
     def block(b):
@@ -82,40 +115,18 @@
     own_x.start()
     for device in group:
         remote(meta.at[o], meta.at[o], s_meta, r_meta, device).start()
+    for k in (2, 3, 1, 0):
+        post(0, 0, k)
+
+    wait(meta.at[0:7], r_meta)
+    named = [meta[:, k, :] for k in range(10)]
+    gates = [meta[:, 16 + k, :] for k in range(10)]
 
     def find(column, k, table=None):
         at = jnp.int32(0)
         for j in range(8):
             at = at + jnp.where(lane[column * 8 + j] == k, j if table is None else table[column * 8 + j], 0)
         return at
-
-    lanes = [lane[e * 8 + j] for j in range(8)]
-    for i in range(2):
-        for w in range(3):
-            if i == 0:
-                loads[w].wait()
-            for k in (2, 3, 1, 0):
-                n = (i * 3 + w) * 4 + k
-
-                def choose(t, _):
-                    at = pl.multiple_of(t * 64, 64)
-                    kept = big[pl.ds(pl.multiple_of(w * 4096 + at, 64), 64), :]
-                    for j in range(1, 8):
-                        other = big[pl.ds(pl.multiple_of((w * 8 + j) * 512 + at, 64), 64), :]
-                        kept = lax.select(lanes[j] == 2 * tgt[k] + i, other, kept)
-                    stage[n, pl.ds(at, 64), :] = kept
-                    return 0
-
-                lax.fori_loop(0, 8, choose, 0)
-                place = outs[w].at[i, pl.ds(pl.multiple_of(r * 512, 512), 512)]
-                if k:
-                    remote(stage.at[n], place, s_w, r_w.at[i, w, r], dev(e, tgt[k])).start()
-                else:
-                    pltpu.make_async_copy(stage.at[n], place, r_w.at[i, w, r]).start()
-
-    wait(meta.at[0:7], r_meta)
-    named = [meta[:, k, :] for k in range(10)]
-    gates = [meta[:, 16 + k, :] for k in range(10)]
 
     def expert_of(s):
         column = (s // 2) * 2 + xh
@@ -156,7 +167,9 @@
     at = jnp.where(near, jnp.where(rank < 16.0, rank, rank + 16.0), jnp.where(rank < 16.0, rank + 16.0, rank + 24.0))
     row3[...] = jnp.where(hits > 0.5, at, -1.0).reshape(32, 8, 128)
     mask3[...] = mm(mm(any_block, hits16).astype(BF), ones).reshape(32, 8, 128)
-    cnt[g] = mask3[:, 0, :]
+    lanes128 = lax.broadcasted_iota(jnp.int32, (256, 128), 1)
+    counts = jnp.where(((row[:, 0:128] >> 3) == lanes128) & ((row[:, 0:128] & 7) == 0), mask3[...].reshape(256, 128), 0.0)
+    cnt[g] = jnp.broadcast_to(jnp.sum(counts, axis=0, keepdims=True), (8, 128))
 
     def tell(m, _):
         remote(cnt.at[g], cnt.at[g], s_cnt, r_cnt, plane(m // 4, m % 4)).start()
@@ -168,6 +181,8 @@
         x_sends.append(remote(block(b), block(b), s_x.at[n], r_x.at[b], device))
         x_sends[-1].start()
 
+    loads[1].wait()
+    ship(0, 1, (2, 3, 1, 0))
     ob, oi, oa = xh * 4 + tgt[2], (1 - xh) * 4 + tgt[2], (1 - xh) * 4 + r
     wait(block(ob), r_x.at[ob])
     forward(ob, 3, sib)
@@ -224,20 +239,28 @@
         wait(block(b), r_x.at[b])
     for part in (0, 2, 1):
         dispatch(0, part)
+    ship(1, 0, (2, 3, 1, 0))
     wait(block(oa), r_x.at[oa])
     forward(oa, 6, sib)
+    ship(1, 1, (2, 3, 1, 0))
     for b in ((1 - xh) * 4 + tgt[1], (1 - xh) * 4 + tgt[3]):
         wait(block(b), r_x.at[b])
     for part in (0, 2, 1):
         dispatch(1, part)
+    loads[2].wait()
+    order = [(i, k) for k in (1, 0, 2, 3) for i in range(2)]
+    for i, k in order:
+        choose(i, 2, k)
+    for i, k in order:
+        post(i, 2, k)
 
     wait(cnt.at[0:15], r_cnt)
 
     def before(p, total):
         return total + cnt[p] * jnp.where(p < g, 1.0, 0.0)
 
-    seen = lax.fori_loop(0, PEERS, before, jnp.zeros((32, 128), F32))
-    tmp[0:32, :] = seen
+    seen = lax.fori_loop(0, PEERS, before, jnp.zeros((8, 128), F32))
+    tmp[...] = jnp.transpose(jnp.broadcast_to(seen[0:1, :], (128, 128)))
 
     def drop(s, _):
         room = find((s // 2) * 2 + xh, 2 * r + s % 2, cap).astype(F32) - tmp[pl.ds(s, 1), :]
@@ -286,20 +309,15 @@
             lax.fori_loop(0, PEERS, sort, 0)
         else:
             wait(recv.at[0, 0:480], r_d.at[1])
-        fetch = []
         for w in range(2):
             for k in range(4):
                 arrived(i, w, k)
-            fetch.append(pltpu.make_async_copy(outs[w].at[i], wbuf.at[w], l_in.at[w]))
-            fetch[w].start()
-        for copy in fetch:
-            copy.wait()
 
         def part(n, _):
             cols = pl.ds(pl.multiple_of(n * 256, 256), 256)
-            gate = mm(recv[i], wbuf[0, :, cols])
-            up = mm(recv[i], wbuf[1, :, cols])
-            hid[:, cols] = (gate / (1.0 + jnp.exp(-gate)) * up).astype(BF)
+            gate = mm(recv[i], outs[0][i, :, cols])
+            up = mm(recv[i], outs[1][i, :, cols])
+            hid[i, :, cols] = (gate / (1.0 + jnp.exp(-gate)) * up).astype(BF)
             return 0
 
         lax.fori_loop(0, 2, part, 0)
@@ -309,14 +327,10 @@
 
     def produce(i, k):
         arrived(i, 2, k)
-        here = wbuf.at[2, pl.ds(k * 512, 512)]
-        fetch = pltpu.make_async_copy(block_of(i, 2, k), here, l_in.at[2])
-        fetch.start()
-        fetch.wait()
         for n in range(2):
             at = k * 512 + n * 256
             recv[i, :, at : at + 256] = lax.dot_general(
-                hid[...], wbuf[2, at : at + 256, :], (((1,), (1,)), ((), ())), preferred_element_type=F32
+                hid[i], outs[2][i, pl.ds(pl.multiple_of(width[k] * 512 + n * 256, 256), 256), :], (((1,), (1,)), ((), ())), preferred_element_type=F32
             ).astype(BF)
 
         def give_back(m, _):
@@ -388,15 +402,30 @@
         comb[:, pl.ds(pl.multiple_of(width[k] * 512, 512), 512)] = total.astype(BF)
 
     hidden(0)
-    for k in range(4):
-        produce(0, k)
+    produce(0, 0)
+    produce(0, 1)
     hidden(1)
-    for k in range(4):
-        produce(1, k)
+    produce(1, 0)
+    produce(1, 1)
+
+    def late_blocks():
+        for k in (2, 3):
+            for i in range(2):
+                produce(i, k)
+
+    @pl.when(c == 0)
+    def _():
+        late_blocks()
+
     combine(0)
     combine(1)
     to_idle(0)
     to_idle(1)
+
+    @pl.when(c == 1)
+    def _():
+        late_blocks()
+
     combine(2)
     to_idle(2)
     to_busy(2)
@@ -419,7 +448,7 @@
 
 def local(tokens, expert_ids, router_scores, lane_list, capacity, train_gate, train_up, train_down):
     dma = pltpu.SemaphoreType.DMA
-    out_w = jax.ShapeDtypeStruct((2, D, H), BF)
+    out_w = pltpu.VMEM((2, D, H), BF)
     anywhere = pl.BlockSpec(memory_space=pl.ANY)
     vmem = pl.BlockSpec(memory_space=pltpu.VMEM)
     smem = pl.BlockSpec(memory_space=pltpu.SMEM)
@@ -427,17 +456,16 @@
         kernel,
         out_shape=(jax.ShapeDtypeStruct((128, D), BF), out_w, out_w, out_w),
         in_specs=[anywhere, vmem, vmem, smem, smem, anywhere, anywhere, anywhere],
-        out_specs=[vmem, anywhere, anywhere, anywhere],
+        out_specs=[vmem, vmem, vmem, vmem],
         scratch_shapes=[
             pltpu.VMEM((12288, 512), BF),
             pltpu.VMEM((24, 512, 512), BF),
-            pltpu.VMEM((3, D, H), BF),
             pltpu.VMEM((1024, D), BF),
             pltpu.VMEM((6, 256, D), BF),
             pltpu.VMEM((2, ALL, D), BF),
             pltpu.VMEM((384, 1024), BF),
             pltpu.VMEM((2, 1024, ALL), BF),
-            pltpu.VMEM((ALL, H), BF),
+            pltpu.VMEM((2, ALL, H), BF),
             pltpu.VMEM((4, 256, 512), BF),
             pltpu.VMEM((4, 128, 512), BF),
             pltpu.VMEM((4, 128, 512), BF),
@@ -446,14 +474,14 @@
             pltpu.VMEM((32, 8, 128), F32),
             pltpu.VMEM((32, 8, 128), F32),
             pltpu.VMEM((32, 8, 128), F32),
-            pltpu.VMEM((16, 32, 128), F32),
+            pltpu.VMEM((16, 8, 128), F32),
             pltpu.VMEM((128, 128), F32),
             dma((3,)), dma((7,)), dma((8,)), dma, dma, dma, dma((2, 3, 4)), dma, dma,
             dma, dma((2,)), dma, dma((2, 4)),
-            dma((4,)), dma((4,)), dma((4,)), dma((4,)), dma((4,)), dma((4,)), dma, dma((3,)),
+            dma((4,)), dma((4,)), dma((4,)), dma((4,)), dma((4,)), dma((4,)), dma,
         ],
         compiler_params=pltpu.CompilerParams(
-            collective_id=0, has_side_effects=True, vmem_limit_bytes=63 << 20
+            collective_id=0, has_side_effects=True, vmem_limit_bytes=50 << 20
         ),
         name="resync_moe",
     )(

time: 212 us -> 204 us (0.962)
  local copies, waits for them, and re-layouts: 12.2 us -> 6.84 us
  Pallas kernels: 198 us -> 194 us
    unnamed x8 -> x6, local copies, waits for them, and re-layouts: 12.2 us -> 6.84 us
    pallas_call x1, Pallas kernels: 198 us -> 194 us  [local(): pl.pallas_call(kernel, out_shape=(jax.ShapeDtypeStruct((128, D), BF), out...]
where the time goes in v3:
time: 204 us; the launch traced here: 201 us
  Pallas kernels  194 us (95%)
  local copies, waits for them, and re-layouts  6.84 us (3%)
    pallas_call x1, Pallas kernels, local(): pl.pallas_call(kernel, out_shape=(jax.ShapeDtypeStruct((128, D), BF), out...  194 us
    unnamed x6, local copies, waits for them, and re-layouts  6.84 us

profile of v3, /device:TPU:1, one launch (start us, length us, event | category | flops | bytes accessed | tf_op | source)
XLA Modules:
  0.0 201.2 jit_solution(13255331324359243126)
XLA Ops:
  0.6 193.7 %resync_moe.1 = (bf16[128,2048]{1,0:T(8,128)(2,1)}, bf16[2,2048,512]{2,1,0:T(8,128)(2,1)S(1)}, bf16[2,2048,512]{2,1,0:T(8,128)(2,1)S(1)}, bf16[2,2048,512]{2,1,0:T(8,128)(2,1)S(1)}) custom-call(bf16[128,2048]{1,0:T(8,128)(2,1)} %tok.1, s32[10,128]{1,0:T(8,128)} %bitcast.8, f32[10,128]{1,0:T(8,128)} %bitcast.9, s32[256]{0:T(256)} %lane.1, s32[256]{0:T(256)} %cap.1, ...), custom_call_target="tpu_custom_call" | custom-call | tf_op jit(solution)/shard_map/resync_moe/pallas_call | solution.py:455
  194.4 2.0 %copy.16 = bf16[2,2048,512]{2,1,0:T(8,128)(2,1)} copy(bf16[2,2048,512]{2,1,0:T(8,128)(2,1)S(1)} %get-tuple-element.5) | data formatting | bytes 8388608
  196.4 2.0 %copy.17 = bf16[2,2048,512]{2,1,0:T(8,128)(2,1)} copy(bf16[2,2048,512]{2,1,0:T(8,128)(2,1)S(1)} %get-tuple-element.6) | data formatting | bytes 8388608
  198.4 0.0 copy-start
  198.4 2.0 %copy.18 = bf16[2,2048,512]{2,1,0:T(8,128)(2,1)} copy(bf16[2,2048,512]{2,1,0:T(8,128)(2,1)S(1)} %get-tuple-element.7) | data formatting | bytes 8388608
  200.4 0.0 copy-done
  200.4 0.8 copy.19
Async XLA Ops:
  198.4 2.0 %copy-start = (bf16[128,2048]{1,0:T(8,128)(2,1)S(1)}, bf16[128,2048]{1,0:T(8,128)(2,1)}, u32[]{:S(2)}) copy-start(bf16[128,2048]{1,0:T(8,128)(2,1)} %get-tuple-element.12) | copy-start | bytes 1572868

commit v4 on v3

--- a/solution.py
+++ b/solution.py
@@ -354,20 +354,25 @@
         for i in range(2):
             base = (i * 4 + k) * ALL
             wait(big.at[pl.ds(base, 720)], r_ret.at[i, k])
-        for n in range(2):
-            cols = slice(n * 256, n * 256 + 256)
-            total = mm(wmat[0], big[k * ALL : k * ALL + ALL, cols])
-            total = total + mm(wmat[1], big[(4 + k) * ALL : (4 + k) * ALL + ALL, cols])
-            big[partial(k) : partial(k) + 1024, cols] = total.astype(BF)
-        k2 = k
+
+        def sums(core):
+            rows = pl.ds(pl.multiple_of(core * 512, 512), 512)
+            for n in range(2):
+                cols = slice(n * 256, n * 256 + 256)
+                total = mm(wmat[0, rows, :], big[k * ALL : k * ALL + ALL, cols])
+                total = total + mm(wmat[1, rows, :], big[(4 + k) * ALL : (4 + k) * ALL + ALL, cols])
+                big[pl.ds(pl.multiple_of(partial(k) + core * 512, 512), 512), cols] = total.astype(BF)
+
+        sums(1 - c)
         tail.append(
             remote(
                 big.at[pl.ds(pl.multiple_of(partial(k) + (1 - c) * 512, 512), 512)],
-                big.at[pl.ds(sibling(k2), 512)],
-                s_sib.at[k], r_sib.at[k2], sib,
+                big.at[pl.ds(sibling(k), 512)],
+                s_sib.at[k], r_sib.at[k], sib,
             )
         )
         tail[-1].start()
+        sums(c)
 
     def own(k):
         return pl.multiple_of(partial(k) + c * 512, 512)
@@ -377,17 +382,19 @@
         both = big[pl.ds(own(k), 512), :].astype(F32) + big[sibling(k) : sibling(k) + 512, :].astype(F32)
         big[pl.ds(own(k), 512), :] = both.astype(BF)
         k2 = k ^ 2
-        tail.append(
-            remote(
-                big.at[pl.ds(pl.multiple_of(own(k) + (1 - xh) * 256, 256), 256)],
-                idr.at[k2], s_idle.at[k], r_idle.at[k2], idle,
+        for n, part in enumerate((xl, 1 - xl)):
+            tail.append(
+                remote(
+                    big.at[pl.ds(pl.multiple_of(own(k) + (1 - xh) * 256 + part * 128, 128), 128)],
+                    idr.at[k2, pl.ds(pl.multiple_of(part * 128, 128), 128)],
+                    s_idle.at[k, n], r_idle.at[k2, n], idle,
+                )
             )
-        )
-        tail[-1].start()
+            tail[-1].start()
 
     def to_busy(k):
-        wait(idr.at[k], r_idle.at[k])
         there = pl.multiple_of((1 - xl) * 128, 128)
+        wait(idr.at[k, pl.ds(there, 128)], r_idle.at[k, 0])
         mine = big[pl.ds(pl.multiple_of(own(k) + xh * 256 + (1 - xl) * 128, 128), 128), :].astype(F32)
         bout[k] = (mine + idr[k, pl.ds(there, 128), :].astype(F32)).astype(BF)
         k2 = k ^ 2
@@ -395,8 +402,9 @@
         tail[-1].start()
 
     def finish(k):
+        here = pl.multiple_of(xl * 128, 128)
+        wait(idr.at[k, pl.ds(here, 128)], r_idle.at[k, 1])
         wait(binr.at[k], r_busy.at[k])
-        here = pl.multiple_of(xl * 128, 128)
         mine = big[pl.ds(pl.multiple_of(own(k) + xh * 256 + xl * 128, 128), 128), :].astype(F32)
         total = mine + idr[k, pl.ds(here, 128), :].astype(F32) + binr[k].astype(F32)
         comb[:, pl.ds(pl.multiple_of(width[k] * 512, 512), 512)] = total.astype(BF)
@@ -478,7 +486,7 @@
             pltpu.VMEM((128, 128), F32),
             dma((3,)), dma((7,)), dma((8,)), dma, dma, dma, dma((2, 3, 4)), dma, dma,
             dma, dma((2,)), dma, dma((2, 4)),
-            dma((4,)), dma((4,)), dma((4,)), dma((4,)), dma((4,)), dma((4,)), dma,
+            dma((4,)), dma((4,)), dma((4, 2)), dma((4, 2)), dma((4,)), dma((4,)), dma,
         ],
         compiler_params=pltpu.CompilerParams(
             collective_id=0, has_side_effects=True, vmem_limit_bytes=50 << 20

time: 204 us -> 203 us (level); the launches traced: 201 us -> 203 us
  no operation moved by 1% of the time
where the time goes in v4:
time: 203 us
  Pallas kernels  195 us (96%)
  local copies, waits for them, and re-layouts  6.84 us (3%)
    pallas_call x1, Pallas kernels, local(): pl.pallas_call(kernel, out_shape=(jax.ShapeDtypeStruct((128, D), BF), out...  195 us
    unnamed x6, local copies, waits for them, and re-layouts  6.84 us

profile of v4, /device:TPU:1, one launch (start us, length us, event | category | flops | bytes accessed | tf_op | source)
XLA Modules:
  0.0 203.0 jit_solution(17765233128331227278)
XLA Ops:
  0.6 195.5 %resync_moe.1 = (bf16[128,2048]{1,0:T(8,128)(2,1)}, bf16[2,2048,512]{2,1,0:T(8,128)(2,1)S(1)}, bf16[2,2048,512]{2,1,0:T(8,128)(2,1)S(1)}, bf16[2,2048,512]{2,1,0:T(8,128)(2,1)S(1)}) custom-call(bf16[128,2048]{1,0:T(8,128)(2,1)} %tok.1, s32[10,128]{1,0:T(8,128)} %bitcast.8, f32[10,128]{1,0:T(8,128)} %bitcast.9, s32[256]{0:T(256)} %lane.1, s32[256]{0:T(256)} %cap.1, ...), custom_call_target="tpu_custom_call" | custom-call | tf_op jit(solution)/shard_map/resync_moe/pallas_call | solution.py:463
  196.1 2.0 copy.16
  198.2 2.0 copy.17
  200.2 0.0 copy-start
  200.2 2.0 copy.18
  202.2 0.0 copy-done
  202.2 0.8 copy.19
Async XLA Ops:
  200.2 2.0 copy-start
